TPU v7x, 32 devices: a whole 2x2x4 slice. The times are simulated.
32 devices in a mesh: dp: 8 (over z, y), mp: 4 (over x, core).
Axes of the slice: x: 2, y: 2, z: 4, core: 2. Of those that a mesh axis runs over, the one named last changes fastest.
Arguments:
- tokens: bfloat16 [1536, 1152], P('dp'), may hold values from -6 to 6
- doc_lengths: int32 [16, 2], P('dp'), may hold values from 1 to 48, as said below
- cotangent: bfloat16 [1536, 1152], P('dp'), may hold values from -6 to 6
- query_weight: bfloat16 [1152, 1024], P('dp', 'mp'), may hold values from -0.1875 to 0.1875
- key_weight: bfloat16 [1152, 256], P('dp'), may hold values from -0.1875 to 0.1875
- value_weight: bfloat16 [1152, 256], P('dp'), may hold values from -0.1875 to 0.1875
- out_weight: bfloat16 [1024, 1152], P('mp', 'dp'), may hold values from -0.1875 to 0.1875
- gate_weight: bfloat16 [1152, 6912], P('dp', 'mp'), may hold values from -0.1875 to 0.1875
- up_weight: bfloat16 [1152, 6912], P('dp', 'mp'), may hold values from -0.1875 to 0.1875
- down_weight: bfloat16 [6912, 1152], P('mp', 'dp'), may hold values from -0.078125 to 0.078125
- pre_attn_gain: bfloat16 [1152], P('dp'), may hold values from 0.5 to 1.5
- post_attn_gain: bfloat16 [1152], P('dp'), may hold values from 0.5 to 1.5
- pre_ffn_gain: bfloat16 [1152], P('dp'), may hold values from 0.5 to 1.5
- post_ffn_gain: bfloat16 [1152], P('dp'), may hold values from 0.5 to 1.5
- query_gain: bfloat16 [256], P('dp'), may hold values from 0.5 to 1.5
- key_gain: bfloat16 [256], P('dp'), may hold values from 0.5 to 1.5
Outputs:
- mixed: bfloat16 [1536, 1152], P('dp')
- tokens_grad: float32 [1536, 1152], P('dp')
- query_grad: float32 [1152, 1024], P('dp', 'mp')
- key_grad: float32 [1152, 256], P('dp')
- value_grad: float32 [1152, 256], P('dp')
- out_grad: float32 [1024, 1152], P('mp', 'dp')
- gate_grad: float32 [1152, 6912], P('dp', 'mp')
- up_grad: float32 [1152, 6912], P('dp', 'mp')
- down_grad: float32 [6912, 1152], P('mp', 'dp')
- pre_attn_grad: float32 [1152], P('dp')
- post_attn_grad: float32 [1152], P('dp')
- pre_ffn_grad: float32 [1152], P('dp')
- post_ffn_grad: float32 [1152], P('dp')
- query_gain_grad: float32 [256], P('dp')
- key_gain_grad: float32 [256], P('dp')
Inputs may be any that keep to these rules, and one draw needn't show every extreme that they name: Row b of doc_lengths gives the 2 document lengths of buffer b, the buffers of one index of dp being 2 consecutive rows; the documents lie end to end from the buffer's first row, and the rows after them are padding.
All inputs are finite; a program needn't handle non-finite values.
Results may differ from a plain program's by a relative error of at most 0.019.
Values may be sent and summed in bfloat16 or wider, within the bound.
A program may use at most 128 MiB of HBM per device.

v0:
```python
import jax
import jax.numpy as jnp
from jax import lax
from jax.sharding import PartitionSpec as P

WINDOW = 512
EPSILON = 1e-06
THETA_BASE = 10000.0
NEGATIVE = -1e30


def matmul(left_op, right_op):
    return jnp.dot(left_op, right_op, preferred_element_type=jnp.float32)


def inner_rows(left_op, right_op):
    return lax.dot_general(
        left_op, right_op, (((0,), (0,)), ((), ())), preferred_element_type=jnp.float32
    )


def inner_cols(left_op, right_op):
    return lax.dot_general(
        left_op, right_op, (((1,), (1,)), ((), ())), preferred_element_type=jnp.float32
    )


def normed(values, factor):
    return values * lax.rsqrt(jnp.mean(values * values, axis=-1, keepdims=True) + EPSILON) * factor


def rotate(values, cosine, sine_table):
    half_width = values.shape[-1] // 2
    leading = values[..., :half_width]
    trailing = values[..., half_width:]
    return jnp.concatenate(
        [leading * cosine - trailing * sine_table, trailing * cosine + leading * sine_table],
        axis=-1,
    )


def layout(lengths, row_count):
    batches, docs = lengths.shape
    total = batches * row_count
    index = jnp.arange(total, dtype=jnp.int32)
    buffer = index // row_count
    inside = index % row_count
    order = jnp.arange(docs, dtype=jnp.int32)
    ends = jnp.sum(
        jnp.where(order[None, :, None] >= order[None, None, :], lengths[:, None, :], 0), axis=2
    )
    row_ends = jnp.repeat(ends, row_count, axis=0)
    row_lengths = jnp.repeat(lengths, row_count, axis=0)
    passed = inside[:, None] >= row_ends
    segment = jnp.sum(passed.astype(jnp.int32), axis=1)
    begins = jnp.sum(jnp.where(passed, row_lengths, 0), axis=1)
    position = inside - begins
    live_rows = (segment < docs).astype(jnp.float32)
    group = buffer * (docs + 1) + segment
    allowed = (
        (group[:, None] == group[None, :])
        & (index[None, :] <= index[:, None])
        & (index[:, None] - index[None, :] < WINDOW)
    )
    return (position, live_rows, allowed)


def angles(position, head_width):
    half_width = head_width // 2
    frequency = THETA_BASE ** (-2.0 * jnp.arange(half_width, dtype=jnp.float32) / head_width)
    turned = position.astype(jnp.float32)[:, None] * frequency[None, :]
    return (jnp.cos(turned), jnp.sin(turned))


def on_device(
    tokens,
    doc_lengths,
    cotangent,
    query_weight,
    key_weight,
    value_weight,
    out_weight,
    gate_weight,
    up_weight,
    down_weight,
    pre_attn_gain,
    post_attn_gain,
    pre_ffn_gain,
    post_ffn_gain,
    query_gain,
    key_gain,
):
    low = jnp.bfloat16
    full = jnp.float32
    dp = lax.axis_size("dp")
    mp = lax.axis_size("mp")
    shard = lax.axis_index("mp")
    rows, width = tokens.shape
    share = width // dp
    head_width = query_weight.shape[1]
    units = gate_weight.shape[1] // dp
    own_rows = rows // mp
    own = (shard * own_rows, own_rows)
    gain_head = query_gain.shape[0]
    gains = jnp.concatenate(
        [pre_attn_gain, post_attn_gain, pre_ffn_gain, post_ffn_gain, query_gain, key_gain]
    )
    block = jnp.concatenate([query_weight, key_weight, value_weight, out_weight.T], axis=1)
    gains_row = jnp.pad(gains, (0, block.shape[1] - gains.shape[0]))[None]
    packed = jnp.concatenate([block, jnp.pad(gains_row, ((0, 15), (0, 0)))], axis=0)
    packed = lax.all_gather(packed, "dp", axis=0, tiled=False)
    attn_w = packed[:, :share].reshape(width, 4 * head_width)
    qkv_w = attn_w[:, : 3 * head_width]
    out_wt = attn_w[:, 3 * head_width :]
    all_gains = packed[:, share].astype(full)
    gain_one, gain_two, gain_three, gain_four = (
        all_gains[:, i * share : (i + 1) * share].reshape(width) for i in range(4)
    )
    query_g = all_gains[:, 4 * share : 4 * share + gain_head].reshape(head_width)
    key_g = all_gains[:, 4 * share + gain_head : 4 * share + 2 * gain_head].reshape(head_width)
    ffn_block = jnp.stack([gate_weight, up_weight, down_weight.T], axis=0)
    ffn_block = ffn_block.reshape(3, share, dp, units).transpose(2, 1, 0, 3)
    ffn_block = ffn_block.reshape(dp, share, 3 * units)
    ffn_w = lax.all_to_all(ffn_block, "dp", split_axis=0, concat_axis=0, tiled=True)
    ffn_w = ffn_w.reshape(width, 3 * units)
    glu_w = ffn_w[:, : 2 * units]
    down_wt = ffn_w[:, 2 * units :]
    inputs = tokens.astype(full)
    position, live_rows, allowed = layout(doc_lengths, rows // doc_lengths.shape[0])
    cosine, sine_table = angles(position, head_width)
    normed_in = normed(inputs, gain_one).astype(low)
    projected = matmul(normed_in, qkv_w)
    query_pre = projected[:, :head_width]
    key_pre = projected[:, head_width : 2 * head_width]
    value_low = projected[:, 2 * head_width :].astype(low)
    query_low = rotate(normed(query_pre, query_g), cosine, sine_table).astype(low)
    key_low = rotate(normed(key_pre, key_g), cosine, sine_table).astype(low)
    score_scale = head_width ** (-0.5)
    scores = inner_cols(query_low, key_low) * score_scale
    scores = jnp.where(allowed, scores, NEGATIVE)
    row_peak = jnp.max(scores, axis=1, keepdims=True)
    raised = jnp.exp(scores - row_peak)
    attention = raised / jnp.sum(raised, axis=1, keepdims=True)
    attention_low = attention.astype(low)
    attended = matmul(attention_low, value_low).astype(low)
    attn_part = inner_cols(attended, out_wt).astype(low)
    attn_sum = lax.psum_scatter(attn_part, "mp", scatter_dimension=0, tiled=True).astype(full)
    inputs_own = lax.dynamic_slice_in_dim(tokens, *own, axis=0).astype(full)
    upstream = lax.dynamic_slice_in_dim(cotangent, *own, axis=0).astype(full)
    live = lax.dynamic_slice_in_dim(live_rows, *own, axis=0)[:, None]

    def post_norm(values, factor):
        return normed(values, factor) * live

    attn_out, back_two = jax.vjp(post_norm, attn_sum, gain_two)
    middle = inputs_own + attn_out
    normed_mid_own, back_three = jax.vjp(normed, middle, gain_three)
    normed_mid = lax.all_gather(normed_mid_own.astype(low), ("dp", "mp"), axis=0, tiled=True)
    glu_pre = matmul(normed_mid, glu_w)
    gate_proj = glu_pre[:, :units]
    up_proj = glu_pre[:, units:]

    def glu(gate_in, up_in):
        return jax.nn.gelu(gate_in, approximate=True) * up_in

    hidden_full, back_glu = jax.vjp(glu, gate_proj, up_proj)
    hidden = hidden_full.astype(low)
    ffn_part = inner_cols(hidden, down_wt).astype(low)
    ffn_sum = lax.psum_scatter(ffn_part, ("dp", "mp"), scatter_dimension=0, tiled=True).astype(full)
    ffn_out, back_four = jax.vjp(post_norm, ffn_sum, gain_four)
    mixed_own = (middle + ffn_out).astype(low)
    d_ffn_own, grad_four = back_four(upstream)
    d_ffn = lax.all_gather(d_ffn_own.astype(low), ("dp", "mp"), axis=0, tiled=True)
    grad_down_t = inner_rows(d_ffn, hidden)
    d_hidden = matmul(d_ffn, down_wt)
    d_gate, d_up = back_glu(d_hidden)
    d_glu = jnp.concatenate([d_gate.astype(low), d_up.astype(low)], axis=1)
    d_mid_part = inner_cols(d_glu, glu_w).astype(low)
    d_mid = lax.psum_scatter(d_mid_part, ("dp", "mp"), scatter_dimension=0, tiled=True).astype(full)
    grad_glu = inner_rows(normed_mid, d_glu)
    ffn_grad = jnp.concatenate([grad_glu, grad_down_t], axis=1).astype(low)
    ffn_grad = ffn_grad.reshape(dp, share, 3 * units)
    ffn_grad = lax.all_to_all(ffn_grad, "dp", split_axis=0, concat_axis=0, tiled=True)
    ffn_grad = ffn_grad.reshape(dp, share, 3, units).transpose(2, 1, 0, 3)
    ffn_grad = ffn_grad.reshape(3, share, dp * units).astype(full)
    d_mid_add, grad_three = back_three(d_mid)
    d_middle = upstream + d_mid_add
    d_attn_own, grad_two = back_two(d_middle)
    d_attn = lax.all_gather(d_attn_own.astype(low), "mp", axis=0, tiled=True)
    grad_out_t = inner_rows(d_attn, attended)
    d_attended = matmul(d_attn, out_wt).astype(low)
    d_value = inner_rows(attention_low, d_attended).astype(low)
    d_probs = inner_cols(d_attended, value_low)
    d_scores = attention * (d_probs - jnp.sum(attention * d_probs, axis=1, keepdims=True))
    d_scores = d_scores.astype(low)
    d_query_rot = matmul(d_scores, key_low) * score_scale
    d_key_rot = inner_rows(d_scores, query_low) * score_scale

    def turned(values, factor):
        return rotate(normed(values, factor), cosine, sine_table)

    _, back_query = jax.vjp(turned, query_pre, query_g)
    d_query_pre, grad_qgain = back_query(d_query_rot)
    _, back_key = jax.vjp(turned, key_pre, key_g)
    d_key_pre, grad_kgain = back_key(d_key_rot)
    d_qkv = jnp.concatenate([d_query_pre.astype(low), d_key_pre.astype(low), d_value], axis=1)
    d_in_part = inner_cols(d_qkv, qkv_w).astype(low)
    d_in = lax.psum_scatter(d_in_part, "mp", scatter_dimension=0, tiled=True).astype(full)
    grad_qkv = inner_rows(normed_in, d_qkv)
    _, back_one = jax.vjp(normed, inputs_own, gain_one)
    d_in_add, grad_one = back_one(d_in)
    tokens_grad_own = d_middle + d_in_add
    pieces = [
        g.reshape(dp, -1)
        for g in (grad_one, grad_two, grad_three, grad_four, grad_qgain, grad_kgain)
    ]
    gains_grad = jnp.concatenate(pieces, axis=1)
    gains_grad = jnp.pad(gains_grad, ((0, 0), (0, 4 * head_width - gains_grad.shape[1])))
    weights_grad = jnp.concatenate([grad_qkv, grad_out_t], axis=1).reshape(
        dp, share, 4 * head_width
    )
    owned = jnp.concatenate(
        [weights_grad, jnp.pad(gains_grad[:, None], ((0, 0), (0, 15), (0, 0)))], axis=1
    ).astype(low)
    owned = lax.psum_scatter(owned, "dp", scatter_dimension=0, tiled=True)[0].astype(full)
    shared = jnp.concatenate(
        [
            owned[:share, head_width : 3 * head_width].reshape(-1),
            owned[share, : 4 * share + 2 * gain_head],
        ]
    )
    shared = lax.psum(shared, "mp")
    kv_grad = shared[: 2 * share * head_width].reshape(share, 2 * head_width)
    gain_out = shared[2 * share * head_width :]
    mixed = lax.all_gather(mixed_own, "mp", axis=0, tiled=True)
    tokens_grad = lax.all_gather(tokens_grad_own.astype(low), "mp", axis=0, tiled=True).astype(full)
    return (
        mixed,
        tokens_grad,
        owned[:share, :head_width],
        kv_grad[:, :head_width],
        kv_grad[:, head_width:],
        owned[:share, 3 * head_width :].T,
        ffn_grad[0],
        ffn_grad[1],
        ffn_grad[2].T,
        gain_out[:share],
        gain_out[share : 2 * share],
        gain_out[2 * share : 3 * share],
        gain_out[3 * share : 4 * share],
        gain_out[4 * share : 4 * share + gain_head],
        gain_out[4 * share + gain_head :],
    )


def solution(mesh):
    placed = (
        P("dp", None),
        P("dp", None),
        P("dp", None),
        P("dp", "mp"),
        P("dp", None),
        P("dp", None),
        P("mp", "dp"),
        P("dp", "mp"),
        P("dp", "mp"),
        P("mp", "dp"),
        P("dp"),
        P("dp"),
        P("dp"),
        P("dp"),
        P("dp"),
        P("dp"),
    )
    return jax.shard_map(
        on_device,
        mesh=mesh,
        in_specs=placed,
        out_specs=(
            P("dp", None),
            P("dp", None),
            P("dp", "mp"),
            P("dp", None),
            P("dp", None),
            P("mp", "dp"),
            P("dp", "mp"),
            P("dp", "mp"),
            P("mp", "dp"),
            P("dp"),
            P("dp"),
            P("dp"),
            P("dp"),
            P("dp"),
            P("dp"),
        ),
        check_vma=False,
    )
```

profile of v0, /device:TPU:0, one launch (start us, length us, event | category | flops | bytes accessed | tf_op | source)
XLA Modules:
  0.0 653.2 jit_solution(11283578642979378089)
XLA Ops:
  7.2 4.1 concatenate.49
  11.3 1.8 fusion.25
  13.2 0.8 select_reduce_fusion
  14.0 0.8 fusion.94
  15.0 1.2 fusion.16
  16.2 54.4 %all-gather.9.cloned.1.call-done = bf16[1280,1024]{1,0:T(8,128)(2,1)} async-done(((bf16[160,1024]{1,0:T(8,128)(2,1)}), bf16[1280,1024]{1,0:T(8,128)(2,1)}) %all-gather.9.cloned.1.call-update) | async-done | bytes 2621456 | tf_op jit(solution)/shard_map/all_gather | solution.py:111
  70.6 0.9 slice_convert_fusion.3
  71.6 2.1 slice.161
  73.7 0.9 fusion.120
  78.5 1.1 convolution_convert_fusion.6
  80.0 19.5 %reduce-scatter.6.cloned.1.call-done = bf16[48,1152]{1,0:T(8,128)(2,1)} async-done(((bf16[192,1152]{1,0:T(8,128)(2,1)}), bf16[48,1152]{1,0:T(8,128)(2,1)}) %reduce-scatter.6.cloned.1.call-update) | async-done | bytes 110608 | tf_op jit(solution)/shard_map/reduce_scatter | solution.py:147
  99.5 1.0 fusion.48
  101.1 1.2 multiply_reduce_fusion
  102.3 1.7 multiply_convert_fusion.2
  104.1 1.0 stack.12
  105.1 0.9 copy.60
  106.1 0.9 stack.13
  107.0 1.9 copy.61
  109.0 1.0 stack.14
  109.9 0.9 copy.62
  111.2 4.4 maximum_bitcast_fusion
  115.6 3.1 reshape.329
  118.8 61.1 %all_to_all.10 = bf16[8,144,648]{2,1,0:T(8,128)(2,1)S(1)} all-to-all(bf16[8,144,648]{2,1,0:T(8,128)(2,1)} %reshape.329), channel_id=1, replica_groups=mesh['dp'=8,'mp'=4] {'dp'}, dimensions={0} | all-to-all | bytes 2985984 | tf_op jit(solution)/shard_map/all_to_all | solution.py:124
  179.8 4.0 fusion.14
  183.8 1.5 copy-done.7
  185.8 3.3 convolution_convert_fusion
  189.9 100.5 %reduce-scatter.8.cloned.1.call-done = bf16[48,1152]{1,0:T(8,128)(2,1)} async-done(((bf16[1536,1152]{1,0:T(8,128)(2,1)}), bf16[48,1152]{1,0:T(8,128)(2,1)}) %reduce-scatter.8.cloned.1.call-update) | async-done | bytes 110608 | tf_op jit(solution)/shard_map/reduce_scatter | solution.py:169
  290.4 1.0 fusion.50
  291.5 1.2 fusion.41
  292.6 1.7 fusion.44
  294.4 59.1 %all-gather.7.cloned.1.call-done = bf16[1536,1152]{1,0:T(8,128)(2,1)} async-done(((bf16[48,1152]{1,0:T(8,128)(2,1)}), bf16[1536,1152]{1,0:T(8,128)(2,1)}) %all-gather.7.cloned.1.call-update) | async-done | bytes 3538960 | tf_op jit(solution)/shard_map/all_gather | solution.py:173
  353.5 5.0 fusion.11
  358.5 0.8 copy-done.70
  359.3 4.2 convolution_convert_fusion.1
  363.8 101.8 %reduce-scatter.10.cloned.1.call-done = bf16[48,1152]{1,0:T(8,128)(2,1)} async-done(((bf16[1536,1152]{1,0:T(8,128)(2,1)}), bf16[48,1152]{1,0:T(8,128)(2,1)}) %reduce-scatter.10.cloned.1.call-update) | async-done | bytes 110608 | tf_op jit(solution)/shard_map/reduce_scatter | solution.py:179
  465.5 1.2 fusion.42
  466.8 2.0 fusion.39
  469.0 6.8 %all_gather.26 = bf16[192,1152]{1,0:T(8,128)(2,1)S(1)} all-gather(bf16[48,1152]{1,0:T(8,128)(2,1)S(1)} %fusion.45), channel_id=1, replica_groups=mesh['dp'=8,'mp'=4] {'mp'}, dimensions={0}, use_global_device_ids=true | all-gather | bytes 552960 | tf_op jit(solution)/shard_map/all_gather | solution.py:189
  478.3 1.5 convolution_convert_fusion.7
  480.1 1.4 convolution_convert_fusion.4
  481.9 1.8 convolution_convert_fusion.2
  483.7 1.7 pad_maximum_fusion
  485.4 2.9 copy.63
  488.3 11.8 %reduce-scatter.12.cloned.1.call-done = bf16[48,1152]{1,0:T(8,128)(2,1)} async-done(((bf16[192,1152]{1,0:T(8,128)(2,1)}), bf16[48,1152]{1,0:T(8,128)(2,1)}) %reduce-scatter.12.cloned.1.call-update) | async-done | bytes 110608 | tf_op jit(solution)/shard_map/reduce_scatter | solution.py:208
  500.0 1.2 fusion.43
  501.5 1.8 fusion.1
  503.4 3.1 convolution_convert_fusion.5
  506.7 4.1 convolution_convert_fusion.3
  510.8 0.8 copy.65
  512.1 61.5 %all_to_all.11 = bf16[8,144,648]{2,1,0:T(8,128)(2,1)S(1)} all-to-all(bf16[8,144,648]{2,1,0:T(8,128)(2,1)S(1)} %pad_maximum_fusion.1), channel_id=1, replica_groups=mesh['dp'=8,'mp'=4] {'dp'}, dimensions={0} | all-to-all | bytes 2985984 | tf_op jit(solution)/shard_map/all_to_all | solution.py:183
  573.6 4.9 reshape.342
  578.4 8.8 %fusion.116 = (f32[1,144,8,216]{3,0,1,2:T(1,128)S(1)}, f32[1,144,8,216]{3,0,1,2:T(1,128)S(1)}, f32[1,144,8,216]{3,0,1,2:T(1,128)S(1)}) fusion(f32[3,144,8,216]{3,0,1,2:T(4,128)} %bitcast.45), kind=kLoop, calls=%fused_computation.220 | loop fusion | bytes 5971968 | tf_op jit(solution)/shard_map/slice | solution.py:246
  587.9 1.4 squeeze.17
  590.0 1.4 squeeze.16
  592.2 1.4 squeeze.15
  593.6 6.7 %all_gather.24 = bf16[192,1152]{1,0:T(8,128)(2,1)S(1)} all-gather(bf16[48,1152]{1,0:T(8,128)(2,1)S(1)} %copy-done.18), channel_id=1, replica_groups=mesh['dp'=8,'mp'=4] {'mp'}, dimensions={0}, use_global_device_ids=true | all-gather | bytes 552960 | tf_op jit(solution)/shard_map/all_gather | solution.py:235
  600.4 1.0 fusion.47
  601.4 6.8 %all_gather.27 = bf16[192,1152]{1,0:T(8,128)(2,1)S(1)} all-gather(bf16[48,1152]{1,0:T(8,128)(2,1)S(1)} %fusion.47), channel_id=1, replica_groups=mesh['dp'=8,'mp'=4] {'mp'}, dimensions={0}, use_global_device_ids=true | all-gather | bytes 552960 | tf_op jit(solution)/shard_map/all_gather | solution.py:236
  608.2 1.0 convert_element_type.166
  609.2 1.0 bitcast_convert_fusion
  611.9 29.4 %all-reduce.10.cloned.1.call-done = f32[74368]{0:T(1024)} async-done(((f32[74368]{0:T(1024)}), f32[74368]{0:T(1024)}) %all-reduce.10.cloned.1.call-update) | async-done | bytes 297488 | tf_op jit(solution)/shard_map/psum | solution.py:232
  641.3 1.0 slice.183
  643.1 1.3 fusion.117
  644.4 1.5 fusion.118
  (231 shorter events, 16.0 us)
Async XLA Ops:
  7.2 63.4 %all-gather.9.cloned.1.call-start = ((), (), s32[]{:S(2)}) async-start(), calls=%async_computation.15 | async-start | bytes 2949120 | tf_op jit(solution)/shard_map/all_gather | solution.py:111
  13.1 86.4 %reduce-scatter.6.cloned.1.call-start = ((), (), s32[]{:S(2)}) async-start(), calls=%async_computation.7 | async-start | bytes 552960 | tf_op jit(solution)/shard_map/reduce_scatter | solution.py:147
  15.0 60.9 %copy-start.57 = (f32[128]{0:T(128)}, f32[128]{0:T(128)S(1)}, u32[]{:S(2)}) copy-start(f32[128]{0:T(128)S(1)} %multiply_power_fusion) | copy-start | bytes 1540
  16.2 58.7 %copy-start.59 = (f32[192]{0:T(256)}, f32[192]{0:T(256)S(1)}, u32[]{:S(2)}) copy-start(f32[192]{0:T(256)S(1)} %add_rsqrt_fusion) | copy-start | bytes 2308
  16.2 59.7 %copy-start.45 = (f32[192]{0:T(256)}, f32[192]{0:T(256)S(1)}, u32[]{:S(2)}) copy-start(f32[192]{0:T(256)S(1)} %fusion.98) | copy-start | bytes 2308
  71.5 3.3 copy-start.6
  73.6 3.9 copy-start.4
  74.7 1.1 copy-start.35
  74.7 1.0 copy-start.37
  75.5 2.1 copy-start.1
  75.6 1.0 copy-start.47
  75.7 1.0 copy-start.49
  75.7 1.0 copy-start.39
  77.0 27.1 %copy-start.14 = (bf16[144,1728]{1,0:T(8,128)(2,1)S(1)}, bf16[144,1728]{1,0:T(8,128)(2,1)}, u32[]{:S(2)}) copy-start(bf16[144,1728]{1,0:T(8,128)(2,1)} %param.23) | copy-start | bytes 1492996
  79.7 100.1 %all-gather.5.cloned.1.call-start = ((), (), s32[]{:S(2)}) async-start(), calls=%async_computation.8 | async-start | bytes 3649536 | tf_op jit(solution)/shard_map/all_gather | solution.py:158
  79.8 25.3 %copy-start.33 = (f32[48]{0:T(128)}, f32[48]{0:T(128)S(1)}, u32[]{:S(2)}) copy-start(f32[48]{0:T(128)S(1)} %dynamic_slice.10) | copy-start | bytes 580
  101.1 4.0 copy-start.43
  101.1 4.9 copy-start.15
  102.3 2.8 copy-start.65
  102.3 2.8 copy-start.51
  104.1 186.4 %reduce-scatter.8.cloned.1.call-start = ((), (), s32[]{:S(2)}) async-start(), calls=%async_computation.9 | async-start | bytes 3649536 | tf_op jit(solution)/shard_map/reduce_scatter | solution.py:169
  106.0 2.9 copy-start.16
  109.9 1.3 copy-start
  183.8 1.5 copy-start.7
  189.1 102.3 %copy-start.21 = (bf16[192,1152]{1,0:T(8,128)(2,1)S(1)}, bf16[192,1152]{1,0:T(8,128)(2,1)}, u32[]{:S(2)}) copy-start(bf16[192,1152]{1,0:T(8,128)(2,1)} %param.18) | copy-start | bytes 1327108
  189.1 102.3 %copy-start.34 = (f32[48]{0:T(128)S(1)}, f32[48]{0:T(128)}, u32[]{:S(2)}) copy-start(f32[48]{0:T(128)} %copy-done.33) | copy-start | bytes 580
  189.1 164.3 %all-gather.7.cloned.1.call-start = ((), (), s32[]{:S(2)}) async-start(), calls=%async_computation.10 | async-start | bytes 3649536 | tf_op jit(solution)/shard_map/all_gather | solution.py:173
  294.4 171.2 %reduce-scatter.10.cloned.1.call-start = ((), (), s32[]{:S(2)}) async-start(), calls=%async_computation.11 | async-start | bytes 3649536 | tf_op jit(solution)/shard_map/reduce_scatter | solution.py:179
  358.5 5.0 copy-start.68
  363.5 102.0 %copy-start.3 = (bf16[48,1152]{1,0:T(8,128)(2,1)S(1)}, bf16[48,1152]{1,0:T(8,128)(2,1)}, u32[]{:S(2)}) copy-start(bf16[48,1152]{1,0:T(8,128)(2,1)} %reduce-scatter.6.cloned.1.call-done) | copy-start | bytes 331780
  363.5 102.0 %copy-start.44 = (f32[48]{0:T(128)S(1)}, f32[48]{0:T(128)}, u32[]{:S(2)}) copy-start(f32[48]{0:T(128)} %copy-done.43) | copy-start | bytes 580
  363.5 102.0 %copy-start.52 = (f32[48]{0:T(128)S(1)}, f32[48]{0:T(128)}, u32[]{:S(2)}) copy-start(f32[48]{0:T(128)} %copy-done.51) | copy-start | bytes 580
  363.5 103.3 %copy-start.66 = (f32[48]{0:T(128)S(1)}, f32[48]{0:T(128)}, u32[]{:S(2)}) copy-start(f32[48]{0:T(128)} %copy-done.65) | copy-start | bytes 580
  363.5 103.3 %copy-start.11 = (bf16[48,1152]{1,0:T(8,128)(2,1)S(1)}, bf16[48,1152]{1,0:T(8,128)(2,1)}, u32[]{:S(2)}) copy-start(bf16[48,1152]{1,0:T(8,128)(2,1)} %reduce-scatter.8.cloned.1.call-done) | copy-start | bytes 331780
  363.6 105.3 %copy-start.64 = (f32[48]{0:T(128)S(1)}, f32[48]{0:T(128)}, u32[]{:S(2)}) copy-start(f32[48]{0:T(128)} %copy-done.63) | copy-start | bytes 580
  363.6 112.3 %copy-start.5 = (bf16[8,144,1024]{2,1,0:T(8,128)(2,1)S(1)}, bf16[8,144,1024]{2,1,0:T(8,128)(2,1)}, u32[]{:S(2)}) copy-start(bf16[8,144,1024]{2,1,0:T(8,128)(2,1)} %copy-done.4) | copy-start | bytes 7077892
  363.6 136.5 %reduce-scatter.12.cloned.1.call-start = ((), (), s32[]{:S(2)}) async-start(), calls=%async_computation.12 | async-start | bytes 552960 | tf_op jit(solution)/shard_map/reduce_scatter | solution.py:208
  363.7 112.5 %copy-start.13 = (f32[192,192]{0,1:T(8,128)S(1)}, f32[192,192]{0,1:T(8,128)}, u32[]{:S(2)}) copy-start(f32[192,192]{0,1:T(8,128)} %copy-done.12) | copy-start | bytes 442372
  363.7 112.5 %copy-start.54 = (f32[192]{0:T(256)S(1)}, f32[192]{0:T(256)}, u32[]{:S(2)}) copy-start(f32[192]{0:T(256)} %copy-done.53) | copy-start | bytes 2308
  363.8 112.5 %copy-start.56 = (f32[192]{0:T(256)S(1)}, f32[192]{0:T(256)}, u32[]{:S(2)}) copy-start(f32[192]{0:T(256)} %copy-done.55) | copy-start | bytes 2308
  466.8 21.5 %copy-start.61 = (f32[48]{0:T(128)}, f32[48]{0:T(128)S(1)}, u32[]{:S(2)}) copy-start(f32[48]{0:T(128)S(1)} %get-tuple-element.29) | copy-start | bytes 580
  468.9 7.9 %copy-start.8 = (f32[48,1152]{1,0:T(8,128)}, f32[48,1152]{1,0:T(8,128)S(1)}, u32[]{:S(2)}) copy-start(f32[48,1152]{1,0:T(8,128)S(1)} %get-tuple-element.34) | copy-start | bytes 663556
  468.9 7.6 %copy-start.2 = (f32[192,768]{1,0:T(8,128)S(1)}, f32[192,768]{1,0:T(8,128)}, u32[]{:S(2)}) copy-start(f32[192,768]{1,0:T(8,128)} %copy-done.1) | copy-start | bytes 1769476
  475.9 1.2 copy-start.23
  475.9 1.2 copy-start.25
  476.3 1.0 copy-start.46
  476.3 1.0 copy-start.58
  476.3 1.5 copy-start.36
  476.3 1.5 copy-start.38
  476.3 1.5 copy-start.40
  476.3 1.5 copy-start.42
  476.5 1.8 copy-start.67
  476.5 1.5 copy-start.48
  476.5 1.5 copy-start.50
  478.3 1.8 copy-start.20
  478.3 3.6 copy-start.31
  478.3 3.6 copy-start.60
  479.9 129.4 %reduce-scatter.14.cloned.1.call-start = ((), (), s32[]{:S(2)}) async-start(), calls=%async_computation.13 | async-start | bytes 2949120 | tf_op jit(solution)/shard_map/reduce_scatter | solution.py:225
  503.3 3.4 copy-start.69
  503.3 138.0 %all-reduce.10.cloned.1.call-start = ((), (), s32[]{:S(2)}) async-start(), calls=%async_computation.14 | async-start | bytes 598016 | tf_op jit(solution)/shard_map/psum | solution.py:232
  591.5 2.2 copy-start.18
  592.2 8.2 %copy-start.62 = (f32[48]{0:T(128)S(1)}, f32[48]{0:T(128)}, u32[]{:S(2)}) copy-start(f32[48]{0:T(128)} %copy-done.61) | copy-start | bytes 580
  592.2 8.2 %copy-start.9 = (f32[48,1152]{1,0:T(8,128)S(1)}, f32[48,1152]{1,0:T(8,128)}, u32[]{:S(2)}) copy-start(f32[48,1152]{1,0:T(8,128)} %copy-done.8) | copy-start | bytes 663556
  592.2 8.2 %copy-start.17 = (bf16[48,1152]{1,0:T(8,128)(2,1)S(1)}, bf16[48,1152]{1,0:T(8,128)(2,1)}, u32[]{:S(2)}) copy-start(bf16[48,1152]{1,0:T(8,128)(2,1)} %reduce-scatter.12.cloned.1.call-done) | copy-start | bytes 331780
  (16 other events, 12.1 us)
Sparse Core Ops, SparseCore 0:
  13.2 57.3 all-gather.8
  79.8 19.6 reduce-scatter.5
  104.2 70.9 all-gather.4
  189.3 101.1 reduce-scatter.7
  294.5 58.9 all-gather.6
  363.7 101.7 reduce-scatter.9
  480.0 20.0 reduce-scatter.11
  503.6 93.4 reduce-scatter.13
  611.3 29.9 all-reduce.9
where the time goes:
time: 654 us; the launch traced here: 653 us
  waiting for transfers between devices  377 us (58%)
  blocking collectives  143 us (22%)
  local copies, waits for them, and re-layouts  54 us (8%)
  other arithmetic  32.3 us (5%)
  matrix products  31.6 us (5%)
  between operations  15.1 us (2%)
    reduce_scatter x1, waiting for transfers between devices, on_device(): lax.psum_scatter(d_mid_part, ('dp', 'mp'), scatter_dimension=0, tiled=True)  102 us
    reduce_scatter x1, waiting for transfers between devices, on_device(): lax.psum_scatter(ffn_part, ('dp', 'mp'), scatter_dimension=0, tiled=True)  101 us
    all_to_all x1, blocking collectives, on_device(): lax.all_to_all(ffn_grad, 'dp', split_axis=0, concat_axis=0, tiled=True)  61.5 us
    all_to_all x1, blocking collectives, on_device(): lax.all_to_all(ffn_block, 'dp', split_axis=0, concat_axis=0, tiled=True)  61.1 us
    all_gather x1, waiting for transfers between devices, on_device(): lax.all_gather(d_ffn_own.astype(low), ('dp', 'mp'), axis=0, tiled=True)  59.1 us
    all_gather x1, waiting for transfers between devices, on_device(): packed = lax.all_gather(packed, 'dp', axis=0, tiled=False)  54.4 us
    psum x1, waiting for transfers between devices, on_device(): shared = lax.psum(shared, 'mp')  29.4 us
    reduce_scatter x1, waiting for transfers between devices, on_device(): lax.psum_scatter(attn_part, 'mp', scatter_dimension=0, tiled=True)  19.5 us
  transfers between devices with their start and end apart: 9, of which 7 were waited for; matrix products, arithmetic and copies ran while one was open for 9% of the time, Pallas kernels for 0%

commit v1 on v0

--- a/solution.py
+++ b/solution.py
@@ -7,6 +7,22 @@
 EPSILON = 1e-06
 THETA_BASE = 10000.0
 NEGATIVE = -1e30
+
+
+def pairwise_exchange(value, axis, split, join):
+    ways, here = (lax.axis_size(axis), lax.axis_index(axis))
+    width = value.shape[split] // ways
+    dims = list(value.shape)
+    dims[split] = width
+    height = dims[join]
+    dims[join] = height * ways
+    full = jnp.zeros(dims, value.dtype)
+    for mask in range(ways):
+        part = lax.dynamic_slice_in_dim(value, (here ^ mask) * width, width, axis=split)
+        if mask:
+            part = lax.ppermute(part, axis, [(d, d ^ mask) for d in range(ways)])
+        full = lax.dynamic_update_slice_in_dim(full, part, (here ^ mask) * height, axis=join)
+    return full
 
 
 def matmul(left_op, right_op):
@@ -121,7 +137,7 @@
     ffn_block = jnp.stack([gate_weight, up_weight, down_weight.T], axis=0)
     ffn_block = ffn_block.reshape(3, share, dp, units).transpose(2, 1, 0, 3)
     ffn_block = ffn_block.reshape(dp, share, 3 * units)
-    ffn_w = lax.all_to_all(ffn_block, "dp", split_axis=0, concat_axis=0, tiled=True)
+    ffn_w = pairwise_exchange(ffn_block, "dp", 0, 0)
     ffn_w = ffn_w.reshape(width, 3 * units)
     glu_w = ffn_w[:, : 2 * units]
     down_wt = ffn_w[:, 2 * units :]

time: 654 us -> 661 us (1.011)
  blocking collectives: 143 us -> 81.6 us
  waiting for transfers between devices: 377 us -> 420 us
  starting transfers between devices: 0.59 us -> 16.1 us
    all_to_all x1 -> x0, blocking collectives: 61.1 us -> none  [on_device(): lax.all_to_all(ffn_block, 'dp', split_axis=0, concat_axis=0, tiled=True)]
    ppermute x0 -> x7, waiting for transfers between devices: none -> 42.4 us  [pairwise_exchange(): part = lax.ppermute(part, axis, [(d, d ^ mask) for d in range(ways)])]
    ppermute x0 -> x7, starting transfers between devices: none -> 15.3 us  [pairwise_exchange(): part = lax.ppermute(part, axis, [(d, d ^ mask) for d in range(ways)])]
  transfers between devices with their start and end apart: 9 -> 16, of which waited for: 7 -> 10; matrix products, arithmetic and copies ran while one was open for 9% -> 9% of each run, Pallas kernels for 0% -> 0%
where the time goes in v1:
time: 661 us; the launch traced here: 654 us
  waiting for transfers between devices  420 us (64%)
  blocking collectives  81.6 us (12%)
  local copies, waits for them, and re-layouts  56.3 us (9%)
  other arithmetic  33.2 us (5%)
  matrix products  31.6 us (5%)
  starting transfers between devices  16.1 us (2%)
  between operations  15.6 us (2%)
    reduce_scatter x1, waiting for transfers between devices, on_device(): lax.psum_scatter(ffn_part, ('dp', 'mp'), scatter_dimension=0, tiled=True)  101 us
    reduce_scatter x1, waiting for transfers between devices, on_device(): lax.psum_scatter(d_mid_part, ('dp', 'mp'), scatter_dimension=0, tiled=True)  101 us
    all_to_all x1, blocking collectives, on_device(): lax.all_to_all(ffn_grad, 'dp', split_axis=0, concat_axis=0, tiled=True)  61.3 us
    all_gather x1, waiting for transfers between devices, on_device(): lax.all_gather(d_ffn_own.astype(low), ('dp', 'mp'), axis=0, tiled=True)  58.9 us
    all_gather x1, waiting for transfers between devices, on_device(): packed = lax.all_gather(packed, 'dp', axis=0, tiled=False)  54.4 us
    ppermute x7, waiting for transfers between devices, pairwise_exchange(): part = lax.ppermute(part, axis, [(d, d ^ mask) for d in range(ways)])  42.4 us
    psum x1, waiting for transfers between devices, on_device(): shared = lax.psum(shared, 'mp')  29.4 us
    reduce_scatter x1, waiting for transfers between devices, on_device(): lax.psum_scatter(attn_part, 'mp', scatter_dimension=0, tiled=True)  19.5 us
  transfers between devices with their start and end apart: 16, of which 10 were waited for; matrix products, arithmetic and copies ran while one was open for 9% of the time, Pallas kernels for 0%

profile of v1, /device:TPU:0, one launch (start us, length us, event | category | flops | bytes accessed | tf_op | source)
XLA Modules:
  0.0 654.0 jit_solution(6159182421417925014)
XLA Ops:
  7.2 4.1 concatenate.49
  11.3 1.8 fusion.25
  15.0 1.2 fusion.16
  16.2 54.4 %all-gather.9.cloned.1.call-done = bf16[1280,1024]{1,0:T(8,128)(2,1)} async-done(((bf16[160,1024]{1,0:T(8,128)(2,1)}), bf16[1280,1024]{1,0:T(8,128)(2,1)}) %all-gather.9.cloned.1.call-update) | async-done | bytes 2621456 | tf_op jit(solution)/shard_map/all_gather | solution.py:127
  71.6 2.1 slice.161
  78.5 1.1 convolution_convert_fusion.6
  80.0 19.5 %reduce-scatter.6.cloned.1.call-done = bf16[48,1152]{1,0:T(8,128)(2,1)} async-done(((bf16[192,1152]{1,0:T(8,128)(2,1)}), bf16[48,1152]{1,0:T(8,128)(2,1)}) %reduce-scatter.6.cloned.1.call-update) | async-done | bytes 110608 | tf_op jit(solution)/shard_map/reduce_scatter | solution.py:163
  99.5 1.0 fusion.48
  101.1 1.2 multiply_reduce_fusion
  102.3 1.7 multiply_convert_fusion.2
  104.1 1.0 stack.12
  106.0 0.9 stack.13
  107.0 1.9 copy.61
  108.9 1.0 stack.14
  111.2 4.9 maximum_bitcast_fusion
  116.1 3.1 reshape.329
  119.3 1.4 copy-done
  120.8 1.5 collective-permute-start
  122.3 1.5 collective-permute-start.1
  123.8 2.4 collective-permute-start.6
  126.2 1.5 collective-permute-start.5
  127.6 1.5 collective-permute-start.4
  129.1 6.9 %collective-permute-start.2 = (bf16[1,144,648]{2,1,0:T(8,128)(2,1)S(1)}, bf16[1,144,648]{2,1,0:T(8,128)(2,1)S(1)}, u32[]{:S(2)}, u32[]{:S(2)}) collective-permute-start(bf16[1,144,648]{2,1,0:T(8,128)(2,1)S(1)} %get-tuple-element.44), channel_id=1, source_target_pairs={{0,12},{4,8},{8,4},{12,0},{16,28},{20,24},{24,20},{28,16},{1,13},{... | collective-permute-start | bytes 559880 | tf_op jit(solution)/shard_map/ppermute | solution.py:23
  136.2 17.7 %collective-permute-done.2 = bf16[1,144,648]{2,1,0:T(8,128)(2,1)S(1)} collective-permute-done((bf16[1,144,648]{2,1,0:T(8,128)(2,1)S(1)}, bf16[1,144,648]{2,1,0:T(8,128)(2,1)S(1)}, u32[]{:S(2)}, u32[]{:S(2)}) %collective-permute-start.2) | collective-permute-done | bytes 186656 | tf_op jit(solution)/shard_map/ppermute | solution.py:23
  153.9 24.6 %collective-permute-done.3 = bf16[1,144,648]{2,1,0:T(8,128)(2,1)S(1)} collective-permute-done((bf16[1,144,648]{2,1,0:T(8,128)(2,1)S(1)}, bf16[1,144,648]{2,1,0:T(8,128)(2,1)S(1)}, u32[]{:S(2)}, u32[]{:S(2)}) %collective-permute-start.3) | collective-permute-done | bytes 186656 | tf_op jit(solution)/shard_map/ppermute | solution.py:23
  179.0 3.9 fusion.14
  183.0 1.5 copy-done.8
  185.0 3.3 convolution_convert_fusion
  189.1 101.3 %reduce-scatter.8.cloned.1.call-done = bf16[48,1152]{1,0:T(8,128)(2,1)} async-done(((bf16[1536,1152]{1,0:T(8,128)(2,1)}), bf16[48,1152]{1,0:T(8,128)(2,1)}) %reduce-scatter.8.cloned.1.call-update) | async-done | bytes 110608 | tf_op jit(solution)/shard_map/reduce_scatter | solution.py:185
  290.4 1.0 fusion.50
  291.5 1.7 fusion.41
  293.1 1.7 fusion.44
  295.1 58.9 %all-gather.7.cloned.1.call-done = bf16[1536,1152]{1,0:T(8,128)(2,1)} async-done(((bf16[48,1152]{1,0:T(8,128)(2,1)}), bf16[1536,1152]{1,0:T(8,128)(2,1)}) %all-gather.7.cloned.1.call-update) | async-done | bytes 3538960 | tf_op jit(solution)/shard_map/all_gather | solution.py:189
  354.0 5.0 fusion.11
  360.0 4.2 convolution_convert_fusion.1
  365.0 101.1 %reduce-scatter.10.cloned.1.call-done = bf16[48,1152]{1,0:T(8,128)(2,1)} async-done(((bf16[1536,1152]{1,0:T(8,128)(2,1)}), bf16[48,1152]{1,0:T(8,128)(2,1)}) %reduce-scatter.10.cloned.1.call-update) | async-done | bytes 110608 | tf_op jit(solution)/shard_map/reduce_scatter | solution.py:195
  466.2 1.2 fusion.42
  467.5 2.0 fusion.39
  469.7 6.8 %all_gather.26 = bf16[192,1152]{1,0:T(8,128)(2,1)S(1)} all-gather(bf16[48,1152]{1,0:T(8,128)(2,1)S(1)} %fusion.45), channel_id=1, replica_groups=mesh['dp'=8,'mp'=4] {'mp'}, dimensions={0}, use_global_device_ids=true | all-gather | bytes 552960 | tf_op jit(solution)/shard_map/all_gather | solution.py:205
  478.9 1.5 convolution_convert_fusion.7
  480.5 1.4 convolution_convert_fusion.4
  482.3 1.8 convolution_convert_fusion.2
  484.1 1.7 pad_maximum_fusion
  485.8 2.9 copy.63
  488.7 12.0 %reduce-scatter.12.cloned.1.call-done = bf16[48,1152]{1,0:T(8,128)(2,1)} async-done(((bf16[192,1152]{1,0:T(8,128)(2,1)}), bf16[48,1152]{1,0:T(8,128)(2,1)}) %reduce-scatter.12.cloned.1.call-update) | async-done | bytes 110608 | tf_op jit(solution)/shard_map/reduce_scatter | solution.py:224
  500.7 1.2 fusion.43
  502.1 1.8 fusion.1
  504.2 3.0 convolution_convert_fusion.5
  507.5 4.1 convolution_convert_fusion.3
  512.9 61.3 %all_to_all.5 = bf16[8,144,648]{2,1,0:T(8,128)(2,1)S(1)} all-to-all(bf16[8,144,648]{2,1,0:T(8,128)(2,1)S(1)} %pad_maximum_fusion.1), channel_id=1, replica_groups=mesh['dp'=8,'mp'=4] {'dp'}, dimensions={0} | all-to-all | bytes 2985984 | tf_op jit(solution)/shard_map/all_to_all | solution.py:199
  574.2 4.8 reshape.342
  579.0 8.8 %fusion.116 = (f32[1,144,8,216]{3,0,1,2:T(1,128)S(1)}, f32[1,144,8,216]{3,0,1,2:T(1,128)S(1)}, f32[1,144,8,216]{3,0,1,2:T(1,128)S(1)}) fusion(f32[3,144,8,216]{3,0,1,2:T(4,128)} %bitcast.45), kind=kLoop, calls=%fused_computation.235 | loop fusion | bytes 5971968 | tf_op jit(solution)/shard_map/slice | solution.py:262
  588.5 1.4 squeeze.17
  590.6 1.4 squeeze.16
  592.8 1.4 squeeze.15
  594.2 6.7 %all_gather.24 = bf16[192,1152]{1,0:T(8,128)(2,1)S(1)} all-gather(bf16[48,1152]{1,0:T(8,128)(2,1)S(1)} %copy-done.19), channel_id=1, replica_groups=mesh['dp'=8,'mp'=4] {'mp'}, dimensions={0}, use_global_device_ids=true | all-gather | bytes 552960 | tf_op jit(solution)/shard_map/all_gather | solution.py:251
  600.9 1.0 fusion.47
  602.0 6.8 %all_gather.27 = bf16[192,1152]{1,0:T(8,128)(2,1)S(1)} all-gather(bf16[48,1152]{1,0:T(8,128)(2,1)S(1)} %fusion.47), channel_id=1, replica_groups=mesh['dp'=8,'mp'=4] {'mp'}, dimensions={0}, use_global_device_ids=true | all-gather | bytes 552960 | tf_op jit(solution)/shard_map/all_gather | solution.py:252
  608.8 1.0 convert_element_type.166
  609.8 1.0 bitcast_convert_fusion
  612.5 29.4 %all-reduce.10.cloned.1.call-done = f32[74368]{0:T(1024)} async-done(((f32[74368]{0:T(1024)}), f32[74368]{0:T(1024)}) %all-reduce.10.cloned.1.call-update) | async-done | bytes 297488 | tf_op jit(solution)/shard_map/psum | solution.py:248
  641.9 1.0 slice.183
  643.6 1.3 fusion.117
  645.0 1.5 fusion.118
  (267 shorter events, 24.5 us)
Async XLA Ops:
  7.2 63.4 %all-gather.9.cloned.1.call-start = ((), (), s32[]{:S(2)}) async-start(), calls=%async_computation.14 | async-start | bytes 2949120 | tf_op jit(solution)/shard_map/all_gather | solution.py:127
  13.1 86.4 %reduce-scatter.6.cloned.1.call-start = ((), (), s32[]{:S(2)}) async-start(), calls=%async_computation.6 | async-start | bytes 552960 | tf_op jit(solution)/shard_map/reduce_scatter | solution.py:163
  15.0 60.9 %copy-start.64 = (f32[128]{0:T(128)}, f32[128]{0:T(128)S(1)}, u32[]{:S(2)}) copy-start(f32[128]{0:T(128)S(1)} %multiply_power_fusion) | copy-start | bytes 1540
  16.2 58.6 %copy-start.66 = (f32[192]{0:T(256)}, f32[192]{0:T(256)S(1)}, u32[]{:S(2)}) copy-start(f32[192]{0:T(256)S(1)} %add_rsqrt_fusion) | copy-start | bytes 2308
  16.2 59.7 %copy-start.50 = (f32[192]{0:T(256)}, f32[192]{0:T(256)S(1)}, u32[]{:S(2)}) copy-start(f32[192]{0:T(256)S(1)} %fusion.98) | copy-start | bytes 2308
  71.5 3.3 copy-start.7
  73.6 3.9 copy-start.5
  75.4 2.1 copy-start.2
  76.9 27.1 %copy-start.15 = (bf16[144,1728]{1,0:T(8,128)(2,1)S(1)}, bf16[144,1728]{1,0:T(8,128)(2,1)}, u32[]{:S(2)}) copy-start(bf16[144,1728]{1,0:T(8,128)(2,1)} %param.23) | copy-start | bytes 1492996
  79.6 99.4 %all-gather.5.cloned.1.call-start = ((), (), s32[]{:S(2)}) async-start(), calls=%async_computation.7 | async-start | bytes 3649536 | tf_op jit(solution)/shard_map/all_gather | solution.py:174
  79.8 25.3 %copy-start.36 = (f32[48]{0:T(128)}, f32[48]{0:T(128)S(1)}, u32[]{:S(2)}) copy-start(f32[48]{0:T(128)S(1)} %dynamic_slice.34) | copy-start | bytes 580
  101.1 4.0 copy-start.48
  101.1 4.9 copy-start.16
  102.3 2.8 copy-start.70
  102.3 2.8 copy-start.56
  104.0 186.4 %reduce-scatter.8.cloned.1.call-start = ((), (), s32[]{:S(2)}) async-start(), calls=%async_computation.8 | async-start | bytes 3649536 | tf_op jit(solution)/shard_map/reduce_scatter | solution.py:185
  106.0 2.9 copy-start.17
  120.8 8.4 %collective-permute-start = (bf16[1,144,648]{2,1,0:T(8,128)(2,1)S(1)}, bf16[1,144,648]{2,1,0:T(8,128)(2,1)S(1)}, u32[]{:S(2)}, u32[]{:S(2)}) collective-permute-start(bf16[1,144,648]{2,1,0:T(8,128)(2,1)S(1)} %get-tuple-element.46), channel_id=1, source_target_pairs={{0,4},{4,0},{8,12},{12,8},{16,20},{20,16},{24,28},{28,24},{1,5},{5... | collective-permute-start | bytes 559880 | tf_op jit(solution)/shard_map/ppermute | solution.py:23
  122.3 13.8 %collective-permute-start.1 = (bf16[1,144,648]{2,1,0:T(8,128)(2,1)S(1)}, bf16[1,144,648]{2,1,0:T(8,128)(2,1)S(1)}, u32[]{:S(2)}, u32[]{:S(2)}) collective-permute-start(bf16[1,144,648]{2,1,0:T(8,128)(2,1)S(1)} %get-tuple-element.45), channel_id=1, source_target_pairs={{0,8},{4,12},{8,0},{12,4},{16,24},{20,28},{24,16},{28,20},{1,9},{5... | collective-permute-start | bytes 559880 | tf_op jit(solution)/shard_map/ppermute | solution.py:23
  123.8 54.9 %collective-permute-start.6 = (bf16[1,144,648]{2,1,0:T(8,128)(2,1)S(1)}, bf16[1,144,648]{2,1,0:T(8,128)(2,1)S(1)}, u32[]{:S(2)}, u32[]{:S(2)}) collective-permute-start(bf16[1,144,648]{2,1,0:T(8,128)(2,1)S(1)} %get-tuple-element.40), channel_id=1, source_target_pairs={{0,28},{4,24},{8,20},{12,16},{16,12},{20,8},{24,4},{28,0},{1,29},{... | collective-permute-start | bytes 559880 | tf_op jit(solution)/shard_map/ppermute | solution.py:23
  126.2 52.5 %collective-permute-start.5 = (bf16[1,144,648]{2,1,0:T(8,128)(2,1)S(1)}, bf16[1,144,648]{2,1,0:T(8,128)(2,1)S(1)}, u32[]{:S(2)}, u32[]{:S(2)}) collective-permute-start(bf16[1,144,648]{2,1,0:T(8,128)(2,1)S(1)} %get-tuple-element.41), channel_id=1, source_target_pairs={{0,24},{4,28},{8,16},{12,20},{16,8},{20,12},{24,0},{28,4},{1,25},{... | collective-permute-start | bytes 559880 | tf_op jit(solution)/shard_map/ppermute | solution.py:23
  127.6 51.0 %collective-permute-start.4 = (bf16[1,144,648]{2,1,0:T(8,128)(2,1)S(1)}, bf16[1,144,648]{2,1,0:T(8,128)(2,1)S(1)}, u32[]{:S(2)}, u32[]{:S(2)}) collective-permute-start(bf16[1,144,648]{2,1,0:T(8,128)(2,1)S(1)} %get-tuple-element.42), channel_id=1, source_target_pairs={{0,20},{4,16},{8,28},{12,24},{16,4},{20,0},{24,12},{28,8},{1,21},{... | collective-permute-start | bytes 559880 | tf_op jit(solution)/shard_map/ppermute | solution.py:23
  129.1 24.8 %collective-permute-start.2 = (bf16[1,144,648]{2,1,0:T(8,128)(2,1)S(1)}, bf16[1,144,648]{2,1,0:T(8,128)(2,1)S(1)}, u32[]{:S(2)}, u32[]{:S(2)}) collective-permute-start(bf16[1,144,648]{2,1,0:T(8,128)(2,1)S(1)} %get-tuple-element.44), channel_id=1, source_target_pairs={{0,12},{4,8},{8,4},{12,0},{16,28},{20,24},{24,20},{28,16},{1,13},{... | collective-permute-start | bytes 559880 | tf_op jit(solution)/shard_map/ppermute | solution.py:23
  136.1 42.5 %collective-permute-start.3 = (bf16[1,144,648]{2,1,0:T(8,128)(2,1)S(1)}, bf16[1,144,648]{2,1,0:T(8,128)(2,1)S(1)}, u32[]{:S(2)}, u32[]{:S(2)}) collective-permute-start(bf16[1,144,648]{2,1,0:T(8,128)(2,1)S(1)} %get-tuple-element.43), channel_id=1, source_target_pairs={{0,16},{4,20},{8,24},{12,28},{16,0},{20,4},{24,8},{28,12},{1,17},{... | collective-permute-start | bytes 559880 | tf_op jit(solution)/shard_map/ppermute | solution.py:23
  182.9 1.6 copy-start.8
  188.3 103.2 %copy-start.22 = (bf16[192,1152]{1,0:T(8,128)(2,1)S(1)}, bf16[192,1152]{1,0:T(8,128)(2,1)}, u32[]{:S(2)}) copy-start(bf16[192,1152]{1,0:T(8,128)(2,1)} %param.18) | copy-start | bytes 1327108
  188.3 103.2 %copy-start.37 = (f32[48]{0:T(128)S(1)}, f32[48]{0:T(128)}, u32[]{:S(2)}) copy-start(f32[48]{0:T(128)} %copy-done.36) | copy-start | bytes 580
  188.3 165.6 %all-gather.7.cloned.1.call-start = ((), (), s32[]{:S(2)}) async-start(), calls=%async_computation.9 | async-start | bytes 3649536 | tf_op jit(solution)/shard_map/all_gather | solution.py:189
  189.1 169.9 %copy-start.31 = (f32[1152]{0:T(1024)}, f32[1152]{0:T(1024)S(1)}, u32[]{:S(2)}) copy-start(f32[1152]{0:T(1024)S(1)} %mul.587) | copy-start | bytes 13828
  291.5 67.5 %copy-start.58 = (f32[48]{0:T(128)}, f32[48]{0:T(128)S(1)}, u32[]{:S(2)}) copy-start(f32[48]{0:T(128)S(1)} %fusion.105) | copy-start | bytes 580
  294.8 171.3 %reduce-scatter.10.cloned.1.call-start = ((), (), s32[]{:S(2)}) async-start(), calls=%async_computation.10 | async-start | bytes 3649536 | tf_op jit(solution)/shard_map/reduce_scatter | solution.py:195
  364.2 101.9 %copy-start.4 = (bf16[48,1152]{1,0:T(8,128)(2,1)S(1)}, bf16[48,1152]{1,0:T(8,128)(2,1)}, u32[]{:S(2)}) copy-start(bf16[48,1152]{1,0:T(8,128)(2,1)} %reduce-scatter.6.cloned.1.call-done) | copy-start | bytes 331780
  364.2 101.9 %copy-start.38 = (f32[48]{0:T(128)S(1)}, f32[48]{0:T(128)}, u32[]{:S(2)}) copy-start(f32[48]{0:T(128)} %copy-done.36) | copy-start | bytes 580
  364.2 101.9 %copy-start.49 = (f32[48]{0:T(128)S(1)}, f32[48]{0:T(128)}, u32[]{:S(2)}) copy-start(f32[48]{0:T(128)} %copy-done.48) | copy-start | bytes 580
  364.2 101.9 %copy-start.57 = (f32[48]{0:T(128)S(1)}, f32[48]{0:T(128)}, u32[]{:S(2)}) copy-start(f32[48]{0:T(128)} %copy-done.56) | copy-start | bytes 580
  364.3 103.2 %copy-start.71 = (f32[48]{0:T(128)S(1)}, f32[48]{0:T(128)}, u32[]{:S(2)}) copy-start(f32[48]{0:T(128)} %copy-done.70) | copy-start | bytes 580
  364.3 103.2 %copy-start.12 = (bf16[48,1152]{1,0:T(8,128)(2,1)S(1)}, bf16[48,1152]{1,0:T(8,128)(2,1)}, u32[]{:S(2)}) copy-start(bf16[48,1152]{1,0:T(8,128)(2,1)} %reduce-scatter.8.cloned.1.call-done) | copy-start | bytes 331780
  364.3 103.2 %copy-start.32 = (f32[1152]{0:T(1024)S(1)}, f32[1152]{0:T(1024)}, u32[]{:S(2)}) copy-start(f32[1152]{0:T(1024)} %copy-done.31) | copy-start | bytes 13828
  364.3 103.2 %copy-start.59 = (f32[48]{0:T(128)S(1)}, f32[48]{0:T(128)}, u32[]{:S(2)}) copy-start(f32[48]{0:T(128)} %copy-done.58) | copy-start | bytes 580
  364.3 105.3 %copy-start.69 = (f32[48]{0:T(128)S(1)}, f32[48]{0:T(128)}, u32[]{:S(2)}) copy-start(f32[48]{0:T(128)} %copy-done.68) | copy-start | bytes 580
  364.3 112.2 %copy-start.6 = (bf16[8,144,1024]{2,1,0:T(8,128)(2,1)S(1)}, bf16[8,144,1024]{2,1,0:T(8,128)(2,1)}, u32[]{:S(2)}) copy-start(bf16[8,144,1024]{2,1,0:T(8,128)(2,1)} %copy-done.5) | copy-start | bytes 7077892
  364.3 136.3 %reduce-scatter.12.cloned.1.call-start = ((), (), s32[]{:S(2)}) async-start(), calls=%async_computation.11 | async-start | bytes 552960 | tf_op jit(solution)/shard_map/reduce_scatter | solution.py:224
  365.0 111.8 %copy-start.14 = (f32[192,192]{0,1:T(8,128)S(1)}, f32[192,192]{0,1:T(8,128)}, u32[]{:S(2)}) copy-start(f32[192,192]{0,1:T(8,128)} %copy-done.13) | copy-start | bytes 442372
  365.0 111.8 %copy-start.61 = (f32[192]{0:T(256)S(1)}, f32[192]{0:T(256)}, u32[]{:S(2)}) copy-start(f32[192]{0:T(256)} %copy-done.60) | copy-start | bytes 2308
  365.0 111.8 %copy-start.63 = (f32[192]{0:T(256)S(1)}, f32[192]{0:T(256)}, u32[]{:S(2)}) copy-start(f32[192]{0:T(256)} %copy-done.62) | copy-start | bytes 2308
  467.4 21.2 %copy-start.72 = (f32[48]{0:T(128)}, f32[48]{0:T(128)S(1)}, u32[]{:S(2)}) copy-start(f32[48]{0:T(128)S(1)} %get-tuple-element.29) | copy-start | bytes 580
  469.5 7.9 %copy-start.9 = (f32[48,1152]{1,0:T(8,128)}, f32[48,1152]{1,0:T(8,128)S(1)}, u32[]{:S(2)}) copy-start(f32[48,1152]{1,0:T(8,128)S(1)} %get-tuple-element.34) | copy-start | bytes 663556
  469.5 7.6 %copy-start.3 = (f32[192,768]{1,0:T(8,128)S(1)}, f32[192,768]{1,0:T(8,128)}, u32[]{:S(2)}) copy-start(f32[192,768]{1,0:T(8,128)} %copy-done.2) | copy-start | bytes 1769476
  476.9 1.5 copy-start.41
  476.9 1.5 copy-start.43
  476.9 1.5 copy-start.45
  477.1 1.8 copy-start.74
  477.1 1.5 copy-start.53
  477.2 1.5 copy-start.55
  478.9 1.6 copy-start.21
  478.9 3.4 copy-start.34
  478.9 3.4 copy-start.67
  480.5 129.3 %reduce-scatter.14.cloned.1.call-start = ((), (), s32[]{:S(2)}) async-start(), calls=%async_computation.12 | async-start | bytes 2949120 | tf_op jit(solution)/shard_map/reduce_scatter | solution.py:241
  503.9 3.6 copy-start.76
  503.9 137.9 %all-reduce.10.cloned.1.call-start = ((), (), s32[]{:S(2)}) async-start(), calls=%async_computation.13 | async-start | bytes 598016 | tf_op jit(solution)/shard_map/psum | solution.py:248
  592.0 2.2 copy-start.19
  592.7 8.2 %copy-start.73 = (f32[48]{0:T(128)S(1)}, f32[48]{0:T(128)}, u32[]{:S(2)}) copy-start(f32[48]{0:T(128)} %copy-done.72) | copy-start | bytes 580
  592.8 8.2 %copy-start.10 = (f32[48,1152]{1,0:T(8,128)S(1)}, f32[48,1152]{1,0:T(8,128)}, u32[]{:S(2)}) copy-start(f32[48,1152]{1,0:T(8,128)} %copy-done.9) | copy-start | bytes 663556
  592.8 8.2 %copy-start.18 = (bf16[48,1152]{1,0:T(8,128)(2,1)S(1)}, bf16[48,1152]{1,0:T(8,128)(2,1)}, u32[]{:S(2)}) copy-start(bf16[48,1152]{1,0:T(8,128)(2,1)} %reduce-scatter.12.cloned.1.call-done) | copy-start | bytes 331780
  (30 other events, 27.4 us)
Sparse Core Ops, SparseCore 0:
  13.2 57.3 all-gather.8
  79.8 19.6 reduce-scatter.5
  104.1 74.8 all-gather.4
  188.4 101.9 reduce-scatter.7
  295.0 58.9 all-gather.6
  364.5 101.6 reduce-scatter.9
  480.6 20.0 reduce-scatter.11
  504.2 93.0 reduce-scatter.13
  611.8 29.9 all-reduce.9
